TPU v7x, 256 devices: a whole 4x4x8 slice. The times are simulated.
256 devices in a mesh: age: 8 (over z_lo, y), sfh: 32 (over z_hi, x, core).
Axes of the slice: x: 4, y: 4, z: 8 (z_hi: 4, z_lo: 2; z = z_hi * 2 + z_lo), core: 2. Of those that a mesh axis runs over, the one named last changes fastest.
Arguments:
- sfh_weights: bfloat16 [16384, 2048], P('sfh', 'age'), may hold values from 3e-06 to 0.032, as said below
- library: bfloat16 [2048, 5120], P('age', 'sfh'), may hold values from 0.00099 to 100.5, as said below
- kernels: bfloat16 [1280, 160, 64], P(('age', 'sfh')), may hold values from -0.078125 to 0.078125
Outputs:
- photometry: bfloat16 [1280, 16384, 64], P(('age', 'sfh'))
Inputs may be any that keep to these rules, and one draw needn't show every extreme that they name: `sfh_weights`: Positive. `library`: Positive.
All inputs are finite; a program needn't handle non-finite values.
Results may differ from a plain program's by a relative error of at most 0.017.
Values may be sent and summed in bfloat16 or wider, within the bound.
A program may use at most 64 MiB of HBM per device.

v0:
```python
import jax
import jax.numpy as jnp
from jax import lax
from jax.sharding import PartitionSpec as P


def local(sfh_weights, library, kernels):
    partial_sum = jnp.dot(
        sfh_weights,
        lax.all_gather(library, "sfh", axis=1, tiled=True),
        preferred_element_type=jnp.float32,
    )
    composite = lax.psum(partial_sum.astype(jnp.bfloat16), "age")
    windowed = lax.all_to_all(composite, "sfh", split_axis=1, concat_axis=0, tiled=True)
    fluxes = jnp.einsum("sw,zwf->zsf", windowed, kernels, preferred_element_type=jnp.float32)
    return fluxes.astype(jnp.bfloat16)


def solution(mesh):
    placed = (P("sfh", "age"), P("age", "sfh"), P(("age", "sfh"), None, None))
    return jax.shard_map(
        local, mesh=mesh, in_specs=placed, out_specs=P(("age", "sfh"), None, None), check_vma=False
    )
```

profile of v0, /device:TPU:32, one launch (start us, length us, event | category | flops | bytes accessed | tf_op | source)
XLA Modules:
  0.0 353.7 jit_solution(5620788862545590071)
XLA Ops:
  6.5 0.0 copy-start
  6.5 0.0 all-gather.2.cloned.1.call-start
  6.5 0.7 all-gather.2.cloned.1.call-update
  7.3 0.0 all-reduce.2.cloned.1.call-start
  7.3 59.5 %all-gather.2.cloned.1.call-done = bf16[256,5120]{0,1:T(8,128)(2,1)} async-done(((bf16[256,160]{0,1:T(8,128)(2,1)}), bf16[256,5120]{0,1:T(8,128)(2,1)}) %all-gather.2.cloned.1.call-update) | async-done | bytes 2621456 | tf_op jit(solution)/shard_map/all_gather | solution.py:10
  66.8 0.0 copy-done
  66.9 5.7 %convolution_convert_fusion = bf16[512,5120]{1,0:T(8,128)(2,1)} fusion(bf16[512,256]{1,0:T(8,128)(2,1)S(1)} %copy-done, bf16[256,5120]{0,1:T(8,128)(2,1)} %all-gather.2.cloned.1.call-done), kind=kOutput, calls=%fused_computation.1 | convolution fusion | flops 1344798720 | bytes 8126464 | tf_op jit(solution)/shard_map/dot_general | solution.py:8
  72.5 7.9 %copy.5 = bf16[512,5120]{0,1:T(8,128)(2,1)} copy(bf16[512,5120]{1,0:T(8,128)(2,1)} %convolution_convert_fusion) | data formatting | bytes 10485760 | tf_op jit(solution)/shard_map/convert_element_type | solution.py:13
  80.4 0.0 all-reduce.2.cloned.1.call-update
  80.5 128.4 %all-reduce.2.cloned.1.call-done = bf16[512,32,160]{0,2,1:T(8,128)(2,1)} async-done(((bf16[512,32,160]{0,2,1:T(8,128)(2,1)}), bf16[512,32,160]{0,2,1:T(8,128)(2,1)}) %all-reduce.2.cloned.1.call-update) | async-done | bytes 5242896 | tf_op jit(solution)/shard_map/psum | solution.py:13
  208.9 129.6 %all_to_all.19 = bf16[512,32,160]{0,2,1:T(8,128)(2,1)S(1)} all-to-all(bf16[512,32,160]{0,2,1:T(8,128)(2,1)} %all-reduce.2.cloned.1.call-done), channel_id=1, replica_groups=mesh['age'=8,'sfh'=32] {'sfh'}, dimensions={1} | all-to-all | bytes 10485760 | tf_op jit(solution)/shard_map/all_to_all | solution.py:14
  338.5 0.0 copy-start.1
  338.5 0.5 copy.7
  339.1 0.4 copy-done.1
  339.4 2.9 fusion
  342.3 4.6 %convert_bitcast_fusion = bf16[5,16384,64]{1,2,0:T(8,128)(2,1)} fusion(f32[16384,5,64]{0,2,1:T(8,128)S(1)} %bitcast.14), kind=kLoop, calls=%fused_computation | loop fusion | flops 5242880 | bytes 31457280 | tf_op jit(solution)/shard_map/convert_element_type | solution.py:16
Async XLA Ops:
  6.5 60.3 %copy-start = (bf16[512,256]{1,0:T(8,128)(2,1)S(1)}, bf16[512,256]{1,0:T(8,128)(2,1)}, u32[]{:S(2)}) copy-start(bf16[512,256]{1,0:T(8,128)(2,1)} %param.3) | copy-start | bytes 786436
  6.5 60.3 %all-gather.2.cloned.1.call-start = ((), (), s32[]{:S(2)}) async-start(), calls=%async_computation.1 | async-start | bytes 2703360 | tf_op jit(solution)/shard_map/all_gather | solution.py:10
  7.3 201.6 %all-reduce.2.cloned.1.call-start = ((), (), s32[]{:S(2)}) async-start(), calls=%async_computation.2 | async-start | bytes 10485760 | tf_op jit(solution)/shard_map/psum | solution.py:13
  338.5 0.9 copy-start.1
Sparse Core Ops, SparseCore 0:
  9.9 56.9 all-gather.1
  80.6 128.2 all-reduce.1
where the time goes:
time: 354 us
  waiting for transfers between devices  189 us (53%)
  blocking collectives  130 us (37%)
  between operations  13.4 us (4%)
  local copies, waits for them, and re-layouts  8.83 us (2%)
  matrix products  8.54 us (2%)
  other arithmetic  4.6 us (1%)
    all_to_all x1, blocking collectives, local(): lax.all_to_all(composite, 'sfh', split_axis=1, concat_axis=0, tiled=True)  130 us
    psum x1, waiting for transfers between devices, local(): composite = lax.psum(partial_sum.astype(jnp.bfloat16), 'age')  128 us
    all_gather x1, waiting for transfers between devices, local(): lax.all_gather(library, 'sfh', axis=1, tiled=True)  59.5 us
    convert_element_type x1, local copies, waits for them, and re-layouts, local(): composite = lax.psum(partial_sum.astype(jnp.bfloat16), 'age')  7.92 us
  transfers between devices with their start and end apart: 2, of which 2 were waited for; matrix products, arithmetic and copies ran while one was open for 0% of the time, Pallas kernels for 0%

commit v1 on v0

v1 whole, which is shorter than its diff:
```python
import functools

import jax
import jax.numpy as jnp
from jax import lax
from jax.experimental import pallas as pl
from jax.experimental.pallas import tpu as pltpu
from jax.sharding import PartitionSpec as P

MESH = pl.DeviceIdType.MESH

NY, NX, NZH = 4, 4, 4
NAGE, NPLANE = 8, 16
ROWS = 128
HALF = 64
KB = 256
WIN = 160

UNITS = {
    (0, 0): 5.0, (0, 3): 10.5, (0, 1): 10.6, (0, 2): 13.5,
    (3, 0): 15.5, (1, 0): 15.6, (3, 3): 20.5, (3, 1): 20.6,
    (3, 2): 23.0, (2, 0): 23.5, (1, 3): 28.0, (1, 1): 28.1,
    (1, 2): 31.0, (2, 3): 36.0, (2, 1): 36.1, (2, 2): 39.0,
}
PACE = 2.4


def schedule():
    events = []
    now = 8.0
    for unit, arrival in sorted(UNITS.items(), key=lambda item: item[1]):
        events.append((arrival, "weights", unit))
        now = max(now, arrival + 1.5)
        events.append((now, "compose", unit))
        events.append((now + 1.8, "pair", unit))
        events.append((now + 4.0, "ring", unit))
        events.append((now + 9.0, "store", unit))
        now += PACE
    return [(kind, unit) for _, kind, unit in sorted(events)]


def gather_kernel(w_ref, l_ref, out_ref, wall, lib, comp, ssem, rsem, a1_send, a1_recv, lib_sem, out_sem):
    age = lax.axis_index("age")
    sfh = lax.axis_index("sfh")
    zl, y = lax.div(age, NY), lax.rem(age, NY)
    core = lax.rem(sfh, 2)
    plane = lax.div(sfh, 2)
    zh, x = lax.div(plane, NX), lax.rem(plane, NX)

    def at(dzl=0, dy=0, dzh=0, dx=0, dc=0):
        a = lax.rem(zl + dzl, 2) * NY + lax.rem(y + dy, NY)
        s = (lax.rem(zh + dzh, NZH) * NX + lax.rem(x + dx, NX)) * 2 + lax.rem(core + dc, 2)
        return (a, s)

    def plane_at(dz, dx):
        return lax.rem(zh + dz, NZH) * NX + lax.rem(x + dx, NX)

    def position(other, dy):
        return lax.rem(zl + other, 2) * NY + lax.rem(y + dy, NY)

    barrier = pltpu.get_barrier_semaphore()
    partners = [at(dzl, dy, 0, 0, dc) for dzl in range(2) for dy in range(NY) for dc in range(2) if (dzl, dy, dc) != (0, 0, 0)]
    partners += [at(dx=1), at(dx=3), at(dzh=1), at(dzh=3)]
    for partner in partners:
        pl.semaphore_signal(barrier, inc=1, device_id=partner, device_id_type=MESH)
    pl.semaphore_wait(barrier, len(partners))

    copies = {}

    def send(name, src, dst, to):
        index = len(copies)
        copy = pltpu.make_async_remote_copy(
            src_ref=src, dst_ref=dst, send_sem=ssem.at[index], recv_sem=rsem.at[index],
            device_id=to, device_id_type=MESH,
        )
        copy.start()
        copies[name] = copy

    def arrived(*name):
        copies[name].wait_recv()

    for q in range(4):
        for h in range(2):
            r = core * 4 + q
            src = w_ref.at[pl.ds(q * ROWS + h * HALF, HALF)]
            dst = wall.at[plane, h, age]
            mine = jnp.logical_and(core == h, r == age)

            @pl.when(mine)
            def _():
                pltpu.make_async_copy(src, dst, a1_recv.at[age]).start()

            @pl.when(jnp.logical_not(mine))
            def _():
                pltpu.make_async_remote_copy(
                    src_ref=src, dst_ref=dst, send_sem=a1_send.at[q * 2 + h], recv_sem=a1_recv.at[age],
                    device_id=(r, plane * 2 + h), device_id_type=MESH,
                ).start()

    own_lib = pltpu.make_async_copy(l_ref, lib.at[age], lib_sem)
    own_lib.start()
    send(("lib", "z"), l_ref, lib.at[age], at(dzl=1))
    send(("lib", "r0"), l_ref, lib.at[age], at(dy=1))
    send(("lib", "l0"), l_ref, lib.at[age], at(dy=3))
    send(("lib", "r1"), l_ref, lib.at[age], at(dzl=1, dy=1))
    send(("lib", "l1"), l_ref, lib.at[age], at(dzl=1, dy=3))

    def weights(unit):
        dz, dx = unit
        p = plane_at(dz, dx)
        part = [wall.at[p, core, pl.ds(0, 4)], wall.at[p, core, pl.ds(4, 4)]]

        def spread(way, half, to):
            send((way, dz, half), part[half], part[half], to)

        if unit == (0, 0):
            for k in range(NAGE):
                pltpu.make_async_copy(w_ref.at[pl.ds(0, HALF)], wall.at[plane, core, k], a1_recv.at[k]).wait()
            spread("x+", 0, at(dx=1))
            spread("x-", 1, at(dx=3))
            spread("z+", 0, at(dzh=1))
            spread("z-", 1, at(dzh=3))
            spread("x+", 1, at(dx=1))
            spread("x-", 0, at(dx=3))
            spread("z+", 1, at(dzh=1))
            spread("z-", 0, at(dzh=3))
        elif dx == 0:
            first = {3: 0, 1: 1, 2: 0}[dz]
            for half in (first, 1 - first):
                if dz == 3:
                    arrived("z+", 0, half)
                    if half == 0:
                        spread("zf+", 0, at(dzh=1))
                elif dz == 1:
                    arrived("z-", 0, half)
                    if half == 1:
                        spread("zf-", 1, at(dzh=3))
                else:
                    arrived(*(("zf+", 3, 0) if half == 0 else ("zf-", 1, 1)))
                spread("x+", half, at(dx=1))
                spread("x-", half, at(dx=3))
        elif dx == 3:
            arrived("x+", dz, 0)
            spread("xf+", 0, at(dx=1))
            arrived("x+", dz, 1)
        elif dx == 1:
            arrived("x-", dz, 1)
            spread("xf-", 1, at(dx=3))
            arrived("x-", dz, 0)
        else:
            arrived("xf+", dz, 0)
            arrived("xf-", dz, 1)
        send(("core", unit), wall.at[p, core], wall.at[p, core], at(dc=1))

    def block(unit, other, dy):
        return comp.at[plane_at(*unit) * NAGE + position(other, dy)]

    def compose(unit):
        arrived("core", unit)
        p = plane_at(*unit)
        total = jnp.zeros((WIN, ROWS), jnp.float32)
        for k in range(NAGE):
            rows = wall[p, :, k].reshape(ROWS, KB)
            total += lax.dot_general(lib[k], rows, (((1,), (1,)), ((), ())), preferred_element_type=jnp.float32)
        comp[p * NAGE + age] = total.astype(jnp.bfloat16)
        mine = block(unit, 0, 0)
        send(("z", unit), mine, mine, at(dzl=1))
        send(("r0", unit), mine, mine, at(dy=1))
        send(("l0", unit), mine, mine, at(dy=3))

    def pair(unit):
        arrived("z", unit)
        theirs = block(unit, 1, 0)
        send(("r1", unit), theirs, theirs, at(dy=1))
        send(("l1", unit), theirs, theirs, at(dy=3))

    def ring(unit):
        arrived("r0", unit)
        left = block(unit, 0, 3)
        send(("f0", unit), left, left, at(dy=1))
        arrived("l1", unit)
        right = block(unit, 1, 1)
        send(("f1", unit), right, right, at(dy=3))

    stores = []

    def store(unit):
        for name in ("l0", "r1", "f0", "f1"):
            arrived(name, unit)
        part = pl.ds(plane_at(*unit) * NAGE, NAGE)
        copy = pltpu.make_async_copy(comp.at[part], out_ref.at[part], out_sem.at[len(stores)])
        copy.start()
        stores.append(copy)

    ready = False
    for kind, unit in schedule():
        if kind == "weights":
            weights(unit)
            if unit == (0, 0):
                arrived("lib", "r0")
                left = lib.at[position(0, 3)]
                send(("lib", "f0"), left, left, at(dy=1))
                arrived("lib", "l1")
                right = lib.at[position(1, 1)]
                send(("lib", "f1"), right, right, at(dy=3))
        elif kind == "compose":
            if not ready:
                own_lib.wait()
                for name in ("z", "l0", "r1", "f0", "f1"):
                    arrived("lib", name)
                ready = True
            compose(unit)
        elif kind == "pair":
            pair(unit)
        elif kind == "ring":
            ring(unit)
        else:
            store(unit)

    for q in range(4):
        for h in range(2):
            mine = jnp.logical_and(core == h, core * 4 + q == age)

            @pl.when(jnp.logical_not(mine))
            def _():
                rows = w_ref.at[pl.ds(q * ROWS + h * HALF, HALF)]
                pltpu.make_async_copy(rows, wall.at[plane, core, 0], a1_send.at[q * 2 + h]).wait()

    for copy in copies.values():
        copy.wait_send()
    for copy in stores:
        copy.wait()


def composites(weights, library_t):
    n_copies = 7 + 30 + 16 + 7 * 16
    return pl.pallas_call(
        gather_kernel,
        out_shape=jax.ShapeDtypeStruct((NPLANE * NAGE, WIN, ROWS), jnp.bfloat16),
        in_specs=[pl.BlockSpec(memory_space=pltpu.VMEM)] * 2,
        out_specs=pl.BlockSpec(memory_space=pl.ANY),
        scratch_shapes=[
            pltpu.VMEM((NPLANE, 2, NAGE, HALF, KB), jnp.bfloat16),
            pltpu.VMEM((NAGE, WIN, KB), jnp.bfloat16),
            pltpu.VMEM((NPLANE * NAGE, WIN, ROWS), jnp.bfloat16),
            pltpu.SemaphoreType.DMA((n_copies,)),
            pltpu.SemaphoreType.DMA((n_copies,)),
            pltpu.SemaphoreType.DMA((8,)),
            pltpu.SemaphoreType.DMA((8,)),
            pltpu.SemaphoreType.DMA,
            pltpu.SemaphoreType.DMA((NPLANE,)),
        ],
        compiler_params=pltpu.CompilerParams(
            collective_id=0, has_side_effects=True, vmem_limit_bytes=40 * 1024 * 1024
        ),
        cost_estimate=pl.CostEstimate(
            flops=2 * 2048 * 2048 * WIN, bytes_accessed=6 * 1024 * 1024, transcendentals=0
        ),
        name="composites",
    )(weights, library_t)


BLOCKS = 16


def photometry_kernel(k_ref, c_ref, o_ref):
    n_z, n_f, n_w = k_ref.shape
    kern = k_ref[...].reshape(n_z * n_f, n_w)
    for b in range(0, BLOCKS, 2):
        cols = jnp.concatenate([c_ref[b], c_ref[b + 1]], axis=1)
        flux = jnp.dot(kern, cols, preferred_element_type=jnp.float32).astype(jnp.bfloat16)
        o_ref[:, :, b * ROWS:(b + 2) * ROWS] = flux.reshape(n_z, n_f, 2 * ROWS)


def photometry(kernels_t, composite):
    n_z, n_f, n_w = kernels_t.shape
    n_blocks = composite.shape[0]
    return pl.pallas_call(
        photometry_kernel,
        grid=(n_blocks // BLOCKS,),
        out_shape=jax.ShapeDtypeStruct((n_z, n_f, n_blocks * ROWS), jnp.bfloat16),
        in_specs=[
            pl.BlockSpec((n_z, n_f, n_w), lambda i: (0, 0, 0)),
            pl.BlockSpec((BLOCKS, n_w, ROWS), lambda i: (i, 0, 0)),
        ],
        out_specs=pl.BlockSpec((n_z, n_f, BLOCKS * ROWS), lambda i: (0, 0, i)),
        compiler_params=pltpu.CompilerParams(vmem_limit_bytes=24 * 1024 * 1024),
        name="photometry",
    )(kernels_t, composite)


def local(sfh_weights, library, kernels):
    composite = composites(sfh_weights, library.T)
    fluxes = photometry(kernels.transpose(0, 2, 1), composite)
    return fluxes.transpose(0, 2, 1)


def solution(mesh):
    placed = (P("sfh", "age"), P("age", "sfh"), P(("age", "sfh"), None, None))
    return jax.shard_map(
        local, mesh=mesh, in_specs=placed, out_specs=P(("age", "sfh"), None, None), check_vma=False
    )
```

time: 354 us -> 115 us (0.32)
  waiting for transfers between devices: 189 us -> 0 us
  blocking collectives: 130 us -> 0 us
  Pallas kernels: 0 us -> 111 us
  between operations: 13.4 us -> 0.02 us
  matrix products: 8.54 us -> 0 us
  local copies, waits for them, and re-layouts: 8.83 us -> 2.75 us
  other arithmetic: 4.6 us -> 0 us
    all_to_all x1 -> x0, blocking collectives: 130 us -> none  [local(): lax.all_to_all(composite, 'sfh', split_axis=1, concat_axis=0, tiled=True)]
    psum x1 -> x0, waiting for transfers between devices: 128 us -> none  [local(): composite = lax.psum(partial_sum.astype(jnp.bfloat16), 'age')]
    pallas_call x0 -> x2, Pallas kernels: none -> 111 us  [the longest x1 104 us: composites(): pl.pallas_call(gather_kernel, out_shape=jax.ShapeDtypeStruct((NPLANE * NA...]
    all_gather x1 -> x0, waiting for transfers between devices: 59.5 us -> none  [local(): lax.all_gather(library, 'sfh', axis=1, tiled=True)]
    convert_element_type x1 -> x0, local copies, waits for them, and re-layouts: 7.92 us -> none  [local(): composite = lax.psum(partial_sum.astype(jnp.bfloat16), 'age')]
    dot_general x1 -> x0, matrix products: 5.66 us -> none  [local(): jnp.dot(sfh_weights, lax.all_gather(library, 'sfh', axis=1, tiled=True),...]
    convert_element_type x1 -> x0, other arithmetic: 4.6 us -> none  [local(): return fluxes.astype(jnp.bfloat16)]
  transfers between devices with their start and end apart: 2 -> 0, of which waited for: 2 -> 0; matrix products, arithmetic and copies ran while one was open for 0% -> 0% of each run, Pallas kernels for 0% -> 0%
where the time goes in v1:
time: 115 us; the launch traced here: 114 us
  Pallas kernels  111 us (97%)
  local copies, waits for them, and re-layouts  2.75 us (2%)
    pallas_call x1, Pallas kernels, composites(): pl.pallas_call(gather_kernel, out_shape=jax.ShapeDtypeStruct((NPLANE * NA...  104 us
    pallas_call x1, Pallas kernels, photometry(): pl.pallas_call(photometry_kernel, grid=(n_blocks // BLOCKS,), out_shape=j...  6.71 us
    unnamed x6, local copies, waits for them, and re-layouts  2.75 us

profile of v1, /device:TPU:32, one launch (start us, length us, event | category | flops | bytes accessed | tf_op | source)
XLA Modules:
  0.0 113.5 jit_solution(11102700744188162503)
XLA Ops:
  0.0 0.0 copy-start
  0.0 0.9 copy-done
  1.0 0.0 copy-start.2
  1.0 0.9 copy-done.2
  1.8 104.1 %composites.1.c_ref = bf16[128,160,128]{2,1,0:T(8,128)(2,1)S(1)} custom-call(bf16[512,256]{1,0:T(8,128)(2,1)S(1)} %copy-done, bf16[160,256]{1,0:T(8,128)(2,1)S(1)} %bitcast.4), custom_call_target="tpu_custom_call" | custom-call | flops 1342177280 | bytes 6291456 | tf_op jit(solution)/shard_map/composites/pallas_call | solution.py:237
  105.9 0.0 copy-start.1
  105.9 0.9 copy-done.1
  106.8 6.7 %photometry.1 = bf16[5,64,16384]{2,1,0:T(8,128)(2,1)} custom-call(bf16[5,64,160]{2,1,0:T(8,128)(2,1)S(1)} %bitcast.3, bf16[128,160,128]{2,1,0:T(8,128)(2,1)S(1)} %composites.1.c_ref), custom_call_target="tpu_custom_call" | custom-call | tf_op jit(solution)/shard_map/photometry/pallas_call | solution.py:278
Async XLA Ops:
  0.0 0.9 copy-start
  1.0 0.9 copy-start.2
  105.9 0.9 copy-start.1

commit v2 on v1

--- a/solution.py
+++ b/solution.py
@@ -16,27 +16,45 @@
 KB = 256
 WIN = 160
 
-UNITS = {
-    (0, 0): 5.0, (0, 3): 10.5, (0, 1): 10.6, (0, 2): 13.5,
-    (3, 0): 15.5, (1, 0): 15.6, (3, 3): 20.5, (3, 1): 20.6,
-    (3, 2): 23.0, (2, 0): 23.5, (1, 3): 28.0, (1, 1): 28.1,
-    (1, 2): 31.0, (2, 3): 36.0, (2, 1): 36.1, (2, 2): 39.0,
+SENT = {
+    "x+": [((0, 0), 0), ((0, 0), 1), ((0, 3), 0), ((3, 0), 0), ((3, 0), 1), ((3, 3), 0),
+           ((1, 0), 0), ((1, 0), 1), ((1, 3), 0), ((2, 0), 0), ((2, 0), 1), ((2, 3), 0)],
+    "x-": [((0, 0), 1), ((0, 0), 0), ((0, 1), 1), ((1, 0), 1), ((1, 0), 0), ((1, 1), 1),
+           ((3, 0), 1), ((3, 0), 0), ((3, 1), 1), ((2, 0), 1), ((2, 0), 0), ((2, 1), 1)],
+    "z+": [((0, 0), 0), ((0, 0), 1), ((3, 0), 0)],
+    "z-": [((0, 0), 1), ((0, 0), 0), ((1, 0), 1)],
 }
-PACE = 2.4
+STEP = {"x+": (0, 1), "x-": (0, 3), "z+": (1, 0), "z-": (3, 0)}
+UNITS = [(0, 0), (0, 3), (0, 1), (0, 2), (3, 0), (1, 0), (3, 3), (1, 1),
+         (2, 0), (1, 3), (3, 1), (3, 2), (1, 2), (2, 3), (2, 1), (2, 2)]
+CROSS = ((0, 1), (3, 0), (2, 0), (3, 2), (2, 3))
+AHEAD = 2
+Z_SEND, Z_RECV = (0.0, 0.0, 2.8), (2.8, 3.8, 6.8)
+LIBRARY, FIRST, PACE = 1.0, 2.2, 0.8
+PAIR_LAG, RING_LAG, STORE_LAG = 2.0, 4.0, 6.0
 
 
 def schedule():
     events = []
-    now = 8.0
-    for unit, arrival in sorted(UNITS.items(), key=lambda item: item[1]):
-        events.append((arrival, "weights", unit))
-        now = max(now, arrival + 1.5)
+    for n in range(12):
+        events.append((max(0, n), "send", ("x+", n)))
+        events.append((max(0, n), "send", ("x-", n)))
+        events.append((n + AHEAD - 0.1, "take", ("x+", n)))
+        events.append((n + AHEAD - 0.1, "take", ("x-", n)))
+    for n in range(3):
+        for way in ("z+", "z-"):
+            events.append((Z_SEND[n] + 0.05, "send", (way, n)))
+            events.append((Z_RECV[n], "take", (way, n)))
+    events.append((LIBRARY, "library", "pass"))
+    events.append((FIRST - 0.01, "library", "wait"))
+    for k, unit in enumerate(UNITS):
+        now = FIRST + PACE * k
         events.append((now, "compose", unit))
-        events.append((now + 1.8, "pair", unit))
-        events.append((now + 4.0, "ring", unit))
-        events.append((now + 9.0, "store", unit))
-        now += PACE
-    return [(kind, unit) for _, kind, unit in sorted(events)]
+        events.append((now + PAIR_LAG, "turn" if unit in CROSS else "pair", unit))
+        events.append((now + RING_LAG, "cross" if unit in CROSS else "ring", unit))
+        events.append((now + STORE_LAG, "store", unit))
+    order = sorted(range(len(events)), key=lambda e: events[e][0])
+    return [events[e][1:] for e in order]
 
 
 def gather_kernel(w_ref, l_ref, out_ref, wall, lib, comp, ssem, rsem, a1_send, a1_recv, lib_sem, out_sem):
@@ -105,58 +123,40 @@
     send(("lib", "r1"), l_ref, lib.at[age], at(dzl=1, dy=1))
     send(("lib", "l1"), l_ref, lib.at[age], at(dzl=1, dy=3))
 
-    def weights(unit):
-        dz, dx = unit
-        p = plane_at(dz, dx)
-        part = [wall.at[p, core, pl.ds(0, 4)], wall.at[p, core, pl.ds(4, 4)]]
-
-        def spread(way, half, to):
-            send((way, dz, half), part[half], part[half], to)
-
-        if unit == (0, 0):
-            for k in range(NAGE):
-                pltpu.make_async_copy(w_ref.at[pl.ds(0, HALF)], wall.at[plane, core, k], a1_recv.at[k]).wait()
-            spread("x+", 0, at(dx=1))
-            spread("x-", 1, at(dx=3))
-            spread("z+", 0, at(dzh=1))
-            spread("z-", 1, at(dzh=3))
-            spread("x+", 1, at(dx=1))
-            spread("x-", 0, at(dx=3))
-            spread("z+", 1, at(dzh=1))
-            spread("z-", 0, at(dzh=3))
-        elif dx == 0:
-            first = {3: 0, 1: 1, 2: 0}[dz]
-            for half in (first, 1 - first):
-                if dz == 3:
-                    arrived("z+", 0, half)
-                    if half == 0:
-                        spread("zf+", 0, at(dzh=1))
-                elif dz == 1:
-                    arrived("z-", 0, half)
-                    if half == 1:
-                        spread("zf-", 1, at(dzh=3))
-                else:
-                    arrived(*(("zf+", 3, 0) if half == 0 else ("zf-", 1, 1)))
-                spread("x+", half, at(dx=1))
-                spread("x-", half, at(dx=3))
-        elif dx == 3:
-            arrived("x+", dz, 0)
-            spread("xf+", 0, at(dx=1))
-            arrived("x+", dz, 1)
-        elif dx == 1:
-            arrived("x-", dz, 1)
-            spread("xf-", 1, at(dx=3))
-            arrived("x-", dz, 0)
+    def library(what):
+        if what == "pass":
+            arrived("lib", "r0")
+            left = lib.at[position(0, 3)]
+            send(("lib", "f0"), left, left, at(dy=1))
+            arrived("lib", "l1")
+            right = lib.at[position(1, 1)]
+            send(("lib", "f1"), right, right, at(dy=3))
         else:
-            arrived("xf+", dz, 0)
-            arrived("xf-", dz, 1)
-        send(("core", unit), wall.at[p, core], wall.at[p, core], at(dc=1))
+            own_lib.wait()
+            for name in ("z", "l0", "r1", "f0", "f1"):
+                arrived("lib", name)
+
+    def pass_on(unit, half):
+        part = wall.at[plane_at(*unit), core, pl.ds(half * 4, 4)]
+        send(("core", unit, half), part, part, at(dc=1))
+
+    def send_weights(way, n):
+        unit, half = SENT[way][n]
+        part = wall.at[plane_at(*unit), core, pl.ds(half * 4, 4)]
+        dz, dx = STEP[way]
+        send((way, n), part, part, at(dzh=dz, dx=dx))
+
+    def take_weights(way, n):
+        (dz, dx), half = SENT[way][n]
+        arrived(way, n)
+        pass_on(((dz - STEP[way][0]) % 4, (dx - STEP[way][1]) % 4), half)
 
     def block(unit, other, dy):
         return comp.at[plane_at(*unit) * NAGE + position(other, dy)]
 
     def compose(unit):
-        arrived("core", unit)
+        arrived("core", unit, 0)
+        arrived("core", unit, 1)
         p = plane_at(*unit)
         total = jnp.zeros((WIN, ROWS), jnp.float32)
         for k in range(NAGE):
@@ -182,40 +182,58 @@
         right = block(unit, 1, 1)
         send(("f1", unit), right, right, at(dy=3))
 
+    def turn(unit):
+        right_way = CROSS.index(unit) % 2 == 0
+        arrived("r0", unit)
+        left = block(unit, 0, 3)
+        if right_way:
+            send(("f0", unit), left, left, at(dy=1))
+        send(("zl", unit), left, left, at(dzl=1))
+        arrived("l0", unit)
+        right = block(unit, 0, 1)
+        if not right_way:
+            send(("f0", unit), right, right, at(dy=3))
+        send(("zr", unit), right, right, at(dzl=1))
+
+    def cross(unit):
+        arrived("f0", unit)
+        far = block(unit, 0, 2)
+        send(("zf", unit), far, far, at(dzl=1))
+
     stores = []
 
     def store(unit):
-        for name in ("l0", "r1", "f0", "f1"):
+        for name in ("z", "zl", "zr", "zf") if unit in CROSS else ("l0", "r1", "f0", "f1"):
             arrived(name, unit)
         part = pl.ds(plane_at(*unit) * NAGE, NAGE)
         copy = pltpu.make_async_copy(comp.at[part], out_ref.at[part], out_sem.at[len(stores)])
         copy.start()
         stores.append(copy)
 
-    ready = False
-    for kind, unit in schedule():
-        if kind == "weights":
-            weights(unit)
-            if unit == (0, 0):
-                arrived("lib", "r0")
-                left = lib.at[position(0, 3)]
-                send(("lib", "f0"), left, left, at(dy=1))
-                arrived("lib", "l1")
-                right = lib.at[position(1, 1)]
-                send(("lib", "f1"), right, right, at(dy=3))
+    for k in range(NAGE):
+        pltpu.make_async_copy(w_ref.at[pl.ds(0, HALF)], wall.at[plane, core, k], a1_recv.at[k]).wait()
+    pass_on((0, 0), 0)
+    pass_on((0, 0), 1)
+
+    for kind, what in schedule():
+        if kind == "send":
+            send_weights(*what)
+        elif kind == "take":
+            take_weights(*what)
+        elif kind == "library":
+            library(what)
         elif kind == "compose":
-            if not ready:
-                own_lib.wait()
-                for name in ("z", "l0", "r1", "f0", "f1"):
-                    arrived("lib", name)
-                ready = True
-            compose(unit)
+            compose(what)
         elif kind == "pair":
-            pair(unit)
+            pair(what)
         elif kind == "ring":
-            ring(unit)
+            ring(what)
+        elif kind == "turn":
+            turn(what)
+        elif kind == "cross":
+            cross(what)
         else:
-            store(unit)
+            store(what)
 
     for q in range(4):
         for h in range(2):
@@ -233,11 +251,11 @@
 
 
 def composites(weights, library_t):
-    n_copies = 7 + 30 + 16 + 7 * 16
+    n_copies = 7 + 30 + 32 + 7 * 16
     return pl.pallas_call(
         gather_kernel,
         out_shape=jax.ShapeDtypeStruct((NPLANE * NAGE, WIN, ROWS), jnp.bfloat16),
-        in_specs=[pl.BlockSpec(memory_space=pltpu.VMEM)] * 2,
+        in_specs=[pl.BlockSpec(memory_space=pltpu.HBM)] * 2,
         out_specs=pl.BlockSpec(memory_space=pl.ANY),
         scratch_shapes=[
             pltpu.VMEM((NPLANE, 2, NAGE, HALF, KB), jnp.bfloat16),
@@ -251,7 +269,7 @@
             pltpu.SemaphoreType.DMA((NPLANE,)),
         ],
         compiler_params=pltpu.CompilerParams(
-            collective_id=0, has_side_effects=True, vmem_limit_bytes=40 * 1024 * 1024
+            collective_id=0, has_side_effects=True, vmem_limit_bytes=24 * 1024 * 1024
         ),
         cost_estimate=pl.CostEstimate(
             flops=2 * 2048 * 2048 * WIN, bytes_accessed=6 * 1024 * 1024, transcendentals=0
@@ -260,14 +278,15 @@
     )(weights, library_t)
 
 
-BLOCKS = 16
+BLOCKS = 32
 
 
 def photometry_kernel(k_ref, c_ref, o_ref):
     n_z, n_f, n_w = k_ref.shape
     kern = k_ref[...].reshape(n_z * n_f, n_w)
+    first = pl.program_id(0) * BLOCKS
     for b in range(0, BLOCKS, 2):
-        cols = jnp.concatenate([c_ref[b], c_ref[b + 1]], axis=1)
+        cols = jnp.concatenate([c_ref[first + b], c_ref[first + b + 1]], axis=1)
         flux = jnp.dot(kern, cols, preferred_element_type=jnp.float32).astype(jnp.bfloat16)
         o_ref[:, :, b * ROWS:(b + 2) * ROWS] = flux.reshape(n_z, n_f, 2 * ROWS)
 
@@ -281,7 +300,7 @@
         out_shape=jax.ShapeDtypeStruct((n_z, n_f, n_blocks * ROWS), jnp.bfloat16),
         in_specs=[
             pl.BlockSpec((n_z, n_f, n_w), lambda i: (0, 0, 0)),
-            pl.BlockSpec((BLOCKS, n_w, ROWS), lambda i: (i, 0, 0)),
+            pl.BlockSpec(memory_space=pltpu.VMEM),
         ],
         out_specs=pl.BlockSpec((n_z, n_f, BLOCKS * ROWS), lambda i: (0, 0, i)),
         compiler_params=pltpu.CompilerParams(vmem_limit_bytes=24 * 1024 * 1024),

time: 115 us -> 84.5 us (0.73)
  Pallas kernels: 111 us -> 81.4 us
    pallas_call x1, Pallas kernels: 104 us -> 75.9 us  [composites(): pl.pallas_call(gather_kernel, out_shape=jax.ShapeDtypeStruct((NPLANE * NA...]
    pallas_call x1, Pallas kernels: 6.71 us -> 5.52 us  [photometry(): pl.pallas_call(photometry_kernel, grid=(n_blocks // BLOCKS,), out_shape=j...]
where the time goes in v2:
time: 84.5 us; the launch traced here: 84.2 us
  Pallas kernels  81.4 us (96%)
  local copies, waits for them, and re-layouts  2.75 us (3%)
    pallas_call x1, Pallas kernels, composites(): pl.pallas_call(gather_kernel, out_shape=jax.ShapeDtypeStruct((NPLANE * NA...  75.9 us
    pallas_call x1, Pallas kernels, photometry(): pl.pallas_call(photometry_kernel, grid=(n_blocks // BLOCKS,), out_shape=j...  5.52 us
    unnamed x6, local copies, waits for them, and re-layouts  2.75 us

profile of v2, /device:TPU:32, one launch (start us, length us, event | category | flops | bytes accessed | tf_op | source)
XLA Modules:
  0.0 84.2 jit_solution(13703916555266406123)
XLA Ops:
  0.0 0.0 copy-start
  0.0 0.9 %copy-done = bf16[512,256]{1,0:T(8,128)(2,1)S(1)} copy-done((bf16[512,256]{1,0:T(8,128)(2,1)S(1)}, bf16[512,256]{1,0:T(8,128)(2,1)}, u32[]{:S(2)}) %copy-start) | copy-done | bytes 262168
  1.0 0.0 copy-start.2
  1.0 0.9 %copy-done.2 = bf16[256,160]{0,1:T(8,128)(2,1)S(1)} copy-done((bf16[256,160]{0,1:T(8,128)(2,1)S(1)}, bf16[256,160]{0,1:T(8,128)(2,1)}, u32[]{:S(2)}) %copy-start.2) | copy-done | bytes 81944
  1.8 75.9 %composites.1.c_ref = bf16[128,160,128]{2,1,0:T(8,128)(2,1)S(1)} custom-call(bf16[512,256]{1,0:T(8,128)(2,1)S(1)} %copy-done, bf16[160,256]{1,0:T(8,128)(2,1)S(1)} %bitcast.4), custom_call_target="tpu_custom_call" | custom-call | flops 1342177280 | bytes 6291456 | tf_op jit(solution)/shard_map/composites/pallas_call | solution.py:255
  77.7 0.0 copy-start.1
  77.7 0.9 %copy-done.1 = bf16[5,160,64]{1,2,0:T(8,128)(2,1)S(1)} copy-done((bf16[5,160,64]{1,2,0:T(8,128)(2,1)S(1)}, bf16[5,160,64]{1,2,0:T(8,128)(2,1)}, u32[]{:S(2)}) %copy-start.1) | copy-done | bytes 102424
  78.6 5.5 %photometry.1 = bf16[5,64,16384]{2,1,0:T(8,128)(2,1)} custom-call(bf16[5,64,160]{2,1,0:T(8,128)(2,1)S(1)} %bitcast.3, bf16[128,160,128]{2,1,0:T(8,128)(2,1)S(1)} %composites.1.c_ref), custom_call_target="tpu_custom_call" | custom-call | tf_op jit(solution)/shard_map/photometry/pallas_call | solution.py:297
Async XLA Ops:
  0.0 0.9 %copy-start = (bf16[512,256]{1,0:T(8,128)(2,1)S(1)}, bf16[512,256]{1,0:T(8,128)(2,1)}, u32[]{:S(2)}) copy-start(bf16[512,256]{1,0:T(8,128)(2,1)} %w_ref.1) | copy-start | bytes 786436
  1.0 0.9 %copy-start.2 = (bf16[256,160]{0,1:T(8,128)(2,1)S(1)}, bf16[256,160]{0,1:T(8,128)(2,1)}, u32[]{:S(2)}) copy-start(bf16[256,160]{0,1:T(8,128)(2,1)} %param.4) | copy-start | bytes 245764
  77.7 0.9 %copy-start.1 = (bf16[5,160,64]{1,2,0:T(8,128)(2,1)S(1)}, bf16[5,160,64]{1,2,0:T(8,128)(2,1)}, u32[]{:S(2)}) copy-start(bf16[5,160,64]{1,2,0:T(8,128)(2,1)} %param.5) | copy-start | bytes 307204

commit v3 on v2

--- a/solution.py
+++ b/solution.py
@@ -17,20 +17,21 @@
 WIN = 160
 
 SENT = {
-    "x+": [((0, 0), 0), ((0, 0), 1), ((0, 3), 0), ((3, 0), 0), ((3, 0), 1), ((3, 3), 0),
-           ((1, 0), 0), ((1, 0), 1), ((1, 3), 0), ((2, 0), 0), ((2, 0), 1), ((2, 3), 0)],
-    "x-": [((0, 0), 1), ((0, 0), 0), ((0, 1), 1), ((1, 0), 1), ((1, 0), 0), ((1, 1), 1),
-           ((3, 0), 1), ((3, 0), 0), ((3, 1), 1), ((2, 0), 1), ((2, 0), 0), ((2, 1), 1)],
+    "x+": [((0, 0), 0), ((0, 0), 1), ((0, 3), 0), ((3, 0), 0), ((1, 0), 1), ((3, 0), 1),
+           ((1, 0), 0), ((3, 3), 0), ((1, 3), 0), ((2, 0), 0), ((2, 0), 1), ((2, 3), 0)],
+    "x-": [((0, 0), 1), ((0, 0), 0), ((0, 1), 1), ((1, 0), 1), ((3, 0), 0), ((1, 0), 0),
+           ((3, 0), 1), ((1, 1), 1), ((3, 1), 1), ((2, 0), 1), ((2, 0), 0), ((2, 1), 1)],
     "z+": [((0, 0), 0), ((0, 0), 1), ((3, 0), 0)],
     "z-": [((0, 0), 1), ((0, 0), 0), ((1, 0), 1)],
 }
 STEP = {"x+": (0, 1), "x-": (0, 3), "z+": (1, 0), "z-": (3, 0)}
 UNITS = [(0, 0), (0, 3), (0, 1), (0, 2), (3, 0), (1, 0), (3, 3), (1, 1),
-         (2, 0), (1, 3), (3, 1), (3, 2), (1, 2), (2, 3), (2, 1), (2, 2)]
-CROSS = ((0, 1), (3, 0), (2, 0), (3, 2), (2, 3))
+         (1, 3), (3, 1), (2, 0), (3, 2), (1, 2), (2, 3), (2, 1), (2, 2)]
+CROSS = ((0, 1), (3, 0), (1, 1), (3, 1), (3, 2), (2, 3))
 AHEAD = 2
-Z_SEND, Z_RECV = (0.0, 0.0, 2.8), (2.8, 3.8, 6.8)
-LIBRARY, FIRST, PACE = 1.0, 2.2, 0.8
+FAR_FIRST = (2, 1, 3, 0)
+Z_SEND, Z_RECV = (-0.05, 1.0, 2.9), (2.85, 4.85, 8.8)
+LIBRARY, TURN, FIRST, PACE = 0.05, 0.8, 2.2, 0.8
 PAIR_LAG, RING_LAG, STORE_LAG = 2.0, 4.0, 6.0
 
 
@@ -43,9 +44,11 @@
         events.append((n + AHEAD - 0.1, "take", ("x-", n)))
     for n in range(3):
         for way in ("z+", "z-"):
-            events.append((Z_SEND[n] + 0.05, "send", (way, n)))
+            events.append((Z_SEND[n], "send", (way, n)))
             events.append((Z_RECV[n], "take", (way, n)))
+    events += [(0.01, "pass", ((0, 0), half)) for half in range(2)]
     events.append((LIBRARY, "library", "pass"))
+    events.append((TURN, "library", "turn"))
     events.append((FIRST - 0.01, "library", "wait"))
     for k, unit in enumerate(UNITS):
         now = FIRST + PACE * k
@@ -97,10 +100,11 @@
     def arrived(*name):
         copies[name].wait_recv()
 
-    for q in range(4):
+    for n, dy in enumerate(FAR_FIRST):
+        q = lax.rem(y + dy, NY)
+        r = core * 4 + q
         for h in range(2):
-            r = core * 4 + q
-            src = w_ref.at[pl.ds(q * ROWS + h * HALF, HALF)]
+            src = w_ref.at[pl.ds(pl.multiple_of(q * ROWS + h * HALF, HALF), HALF)]
             dst = wall.at[plane, h, age]
             mine = jnp.logical_and(core == h, r == age)
 
@@ -111,7 +115,7 @@
             @pl.when(jnp.logical_not(mine))
             def _():
                 pltpu.make_async_remote_copy(
-                    src_ref=src, dst_ref=dst, send_sem=a1_send.at[q * 2 + h], recv_sem=a1_recv.at[age],
+                    src_ref=src, dst_ref=dst, send_sem=a1_send.at[n * 2 + h], recv_sem=a1_recv.at[age],
                     device_id=(r, plane * 2 + h), device_id_type=MESH,
                 ).start()
 
@@ -120,20 +124,23 @@
     send(("lib", "z"), l_ref, lib.at[age], at(dzl=1))
     send(("lib", "r0"), l_ref, lib.at[age], at(dy=1))
     send(("lib", "l0"), l_ref, lib.at[age], at(dy=3))
-    send(("lib", "r1"), l_ref, lib.at[age], at(dzl=1, dy=1))
-    send(("lib", "l1"), l_ref, lib.at[age], at(dzl=1, dy=3))
 
     def library(what):
         if what == "pass":
+            arrived("lib", "z")
+            theirs = lib.at[position(1, 0)]
+            send(("lib", "r1"), theirs, theirs, at(dy=1))
+            send(("lib", "l1"), theirs, theirs, at(dy=3))
             arrived("lib", "r0")
             left = lib.at[position(0, 3)]
             send(("lib", "f0"), left, left, at(dy=1))
+        elif what == "turn":
             arrived("lib", "l1")
             right = lib.at[position(1, 1)]
             send(("lib", "f1"), right, right, at(dy=3))
         else:
             own_lib.wait()
-            for name in ("z", "l0", "r1", "f0", "f1"):
+            for name in ("l0", "r1", "f0", "f1"):
                 arrived("lib", name)
 
     def pass_on(unit, half):
@@ -212,14 +219,13 @@
 
     for k in range(NAGE):
         pltpu.make_async_copy(w_ref.at[pl.ds(0, HALF)], wall.at[plane, core, k], a1_recv.at[k]).wait()
-    pass_on((0, 0), 0)
-    pass_on((0, 0), 1)
-
     for kind, what in schedule():
         if kind == "send":
             send_weights(*what)
         elif kind == "take":
             take_weights(*what)
+        elif kind == "pass":
+            pass_on(*what)
         elif kind == "library":
             library(what)
         elif kind == "compose":
@@ -235,14 +241,14 @@
         else:
             store(what)
 
-    for q in range(4):
+    for n, dy in enumerate(FAR_FIRST):
         for h in range(2):
-            mine = jnp.logical_and(core == h, core * 4 + q == age)
+            mine = jnp.logical_and(core == h, core * 4 + lax.rem(y + dy, NY) == age)
 
             @pl.when(jnp.logical_not(mine))
             def _():
-                rows = w_ref.at[pl.ds(q * ROWS + h * HALF, HALF)]
-                pltpu.make_async_copy(rows, wall.at[plane, core, 0], a1_send.at[q * 2 + h]).wait()
+                rows = w_ref.at[pl.ds(0, HALF)]
+                pltpu.make_async_copy(rows, wall.at[plane, core, 0], a1_send.at[n * 2 + h]).wait()
 
     for copy in copies.values():
         copy.wait_send()

time: 84.5 us -> 81.3 us (0.962); the launches traced: 84.2 us -> 80.1 us
  Pallas kernels: 81.4 us -> 77.3 us
    pallas_call x1, Pallas kernels: 75.9 us -> 71.8 us  [composites(): pl.pallas_call(gather_kernel, out_shape=jax.ShapeDtypeStruct((NPLANE * NA...]
where the time goes in v3:
time: 81.3 us; the launch traced here: 80.1 us
  Pallas kernels  77.3 us (95%)
  local copies, waits for them, and re-layouts  2.75 us (3%)
    pallas_call x1, Pallas kernels, composites(): pl.pallas_call(gather_kernel, out_shape=jax.ShapeDtypeStruct((NPLANE * NA...  71.8 us
    pallas_call x1, Pallas kernels, photometry(): pl.pallas_call(photometry_kernel, grid=(n_blocks // BLOCKS,), out_shape=j...  5.52 us
    unnamed x6, local copies, waits for them, and re-layouts  2.75 us

profile of v3, /device:TPU:32, one launch (start us, length us, event | category | flops | bytes accessed | tf_op | source)
XLA Modules:
  0.0 80.1 jit_solution(1641596957205631089)
XLA Ops:
  0.0 0.0 copy-start
  0.0 0.9 %copy-done = bf16[512,256]{1,0:T(8,128)(2,1)S(1)} copy-done((bf16[512,256]{1,0:T(8,128)(2,1)S(1)}, bf16[512,256]{1,0:T(8,128)(2,1)}, u32[]{:S(2)}) %copy-start) | copy-done | bytes 262168
  1.0 0.0 copy-start.2
  1.0 0.9 %copy-done.2 = bf16[256,160]{0,1:T(8,128)(2,1)S(1)} copy-done((bf16[256,160]{0,1:T(8,128)(2,1)S(1)}, bf16[256,160]{0,1:T(8,128)(2,1)}, u32[]{:S(2)}) %copy-start.2) | copy-done | bytes 81944
  1.8 71.8 %composites.1.c_ref = bf16[128,160,128]{2,1,0:T(8,128)(2,1)S(1)} custom-call(bf16[512,256]{1,0:T(8,128)(2,1)S(1)} %copy-done, bf16[160,256]{1,0:T(8,128)(2,1)S(1)} %bitcast.4), custom_call_target="tpu_custom_call" | custom-call | flops 1342177280 | bytes 6291456 | tf_op jit(solution)/shard_map/composites/pallas_call | solution.py:261
  73.7 0.0 copy-start.1
  73.7 0.9 %copy-done.1 = bf16[5,160,64]{1,2,0:T(8,128)(2,1)S(1)} copy-done((bf16[5,160,64]{1,2,0:T(8,128)(2,1)S(1)}, bf16[5,160,64]{1,2,0:T(8,128)(2,1)}, u32[]{:S(2)}) %copy-start.1) | copy-done | bytes 102424
  74.6 5.5 %photometry.1 = bf16[5,64,16384]{2,1,0:T(8,128)(2,1)} custom-call(bf16[5,64,160]{2,1,0:T(8,128)(2,1)S(1)} %bitcast.3, bf16[128,160,128]{2,1,0:T(8,128)(2,1)S(1)} %composites.1.c_ref), custom_call_target="tpu_custom_call" | custom-call | tf_op jit(solution)/shard_map/photometry/pallas_call | solution.py:303
Async XLA Ops:
  0.0 0.9 %copy-start = (bf16[512,256]{1,0:T(8,128)(2,1)S(1)}, bf16[512,256]{1,0:T(8,128)(2,1)}, u32[]{:S(2)}) copy-start(bf16[512,256]{1,0:T(8,128)(2,1)} %w_ref.1) | copy-start | bytes 786436
  1.0 0.9 %copy-start.2 = (bf16[256,160]{0,1:T(8,128)(2,1)S(1)}, bf16[256,160]{0,1:T(8,128)(2,1)}, u32[]{:S(2)}) copy-start(bf16[256,160]{0,1:T(8,128)(2,1)} %param.4) | copy-start | bytes 245764
  73.7 0.9 %copy-start.1 = (bf16[5,160,64]{1,2,0:T(8,128)(2,1)S(1)}, bf16[5,160,64]{1,2,0:T(8,128)(2,1)}, u32[]{:S(2)}) copy-start(bf16[5,160,64]{1,2,0:T(8,128)(2,1)} %param.5) | copy-start | bytes 307204

commit v4 on v3

--- a/solution.py
+++ b/solution.py
@@ -31,27 +31,37 @@
 AHEAD = 2
 FAR_FIRST = (2, 1, 3, 0)
 Z_SEND, Z_RECV = (-0.05, 1.0, 2.9), (2.85, 4.85, 8.8)
-LIBRARY, TURN, FIRST, PACE = 0.05, 0.8, 2.2, 0.8
+LIBRARY, TURN, FIRST, PACE = 0.05, 0.8, 2.2, 0.65
 PAIR_LAG, RING_LAG, STORE_LAG = 2.0, 4.0, 6.0
+SETTLE = 0.5
 
 
 def schedule():
     events = []
     for n in range(12):
-        events.append((max(0, n), "send", ("x+", n)))
-        events.append((max(0, n), "send", ("x-", n)))
+        events.append((n or -0.24, "send", ("x+", n)))
+        events.append((n or -0.04, "send", ("x-", n)))
         events.append((n + AHEAD - 0.1, "take", ("x+", n)))
         events.append((n + AHEAD - 0.1, "take", ("x-", n)))
     for n in range(3):
         for way in ("z+", "z-"):
-            events.append((Z_SEND[n], "send", (way, n)))
+            early = 0.2 if (way, n) == ("z+", 0) else 0.0
+            events.append((Z_SEND[n] - early, "send", (way, n)))
             events.append((Z_RECV[n], "take", (way, n)))
+    events += [(-0.3, "own", 0), (-0.2, "own", 1)]
     events += [(0.01, "pass", ((0, 0), half)) for half in range(2)]
     events.append((LIBRARY, "library", "pass"))
     events.append((TURN, "library", "turn"))
     events.append((FIRST - 0.01, "library", "wait"))
-    for k, unit in enumerate(UNITS):
-        now = FIRST + PACE * k
+    ready = {}
+    for moment, kind, what in events:
+        if kind == "take":
+            (dz, dx), _ = SENT[what[0]][what[1]]
+            unit = ((dz - STEP[what[0]][0]) % 4, (dx - STEP[what[0]][1]) % 4)
+            ready[unit] = max(ready.get(unit, 0.0), moment + SETTLE)
+    now = FIRST - PACE
+    for unit in UNITS:
+        now = max(now + PACE, ready.get(unit, 0.0))
         events.append((now, "compose", unit))
         events.append((now + PAIR_LAG, "turn" if unit in CROSS else "pair", unit))
         events.append((now + RING_LAG, "cross" if unit in CROSS else "ring", unit))
@@ -60,7 +70,9 @@
     return [events[e][1:] for e in order]
 
 
-def gather_kernel(w_ref, l_ref, out_ref, wall, lib, comp, ssem, rsem, a1_send, a1_recv, lib_sem, out_sem):
+def gather_kernel(
+    w_ref, l_ref, k_ref, out_ref, k_out, wall, lib, comp, ssem, rsem, a1_send, a1_recv, lib_sem, k_sem, out_sem
+):
     age = lax.axis_index("age")
     sfh = lax.axis_index("sfh")
     zl, y = lax.div(age, NY), lax.rem(age, NY)
@@ -121,6 +133,8 @@
 
     own_lib = pltpu.make_async_copy(l_ref, lib.at[age], lib_sem)
     own_lib.start()
+    bring = pltpu.make_async_copy(k_ref, k_out, k_sem)
+    bring.start()
     send(("lib", "z"), l_ref, lib.at[age], at(dzl=1))
     send(("lib", "r0"), l_ref, lib.at[age], at(dy=1))
     send(("lib", "l0"), l_ref, lib.at[age], at(dy=3))
@@ -217,13 +231,17 @@
         copy.start()
         stores.append(copy)
 
-    for k in range(NAGE):
-        pltpu.make_async_copy(w_ref.at[pl.ds(0, HALF)], wall.at[plane, core, k], a1_recv.at[k]).wait()
+    def own(half):
+        for k in range(half * 4, half * 4 + 4):
+            pltpu.make_async_copy(w_ref.at[pl.ds(0, HALF)], wall.at[plane, core, k], a1_recv.at[k]).wait()
+
     for kind, what in schedule():
         if kind == "send":
             send_weights(*what)
         elif kind == "take":
             take_weights(*what)
+        elif kind == "own":
+            own(what)
         elif kind == "pass":
             pass_on(*what)
         elif kind == "library":
@@ -254,15 +272,19 @@
         copy.wait_send()
     for copy in stores:
         copy.wait()
-
-
-def composites(weights, library_t):
+    bring.wait()
+
+
+def composites(weights, library_t, kernels_t):
     n_copies = 7 + 30 + 32 + 7 * 16
     return pl.pallas_call(
         gather_kernel,
-        out_shape=jax.ShapeDtypeStruct((NPLANE * NAGE, WIN, ROWS), jnp.bfloat16),
-        in_specs=[pl.BlockSpec(memory_space=pltpu.HBM)] * 2,
-        out_specs=pl.BlockSpec(memory_space=pl.ANY),
+        out_shape=[
+            jax.ShapeDtypeStruct((NPLANE * NAGE, WIN, ROWS), jnp.bfloat16),
+            jax.ShapeDtypeStruct(kernels_t.shape, kernels_t.dtype),
+        ],
+        in_specs=[pl.BlockSpec(memory_space=pltpu.HBM)] * 3,
+        out_specs=[pl.BlockSpec(memory_space=pl.ANY)] * 2,
         scratch_shapes=[
             pltpu.VMEM((NPLANE, 2, NAGE, HALF, KB), jnp.bfloat16),
             pltpu.VMEM((NAGE, WIN, KB), jnp.bfloat16),
@@ -271,6 +293,7 @@
             pltpu.SemaphoreType.DMA((n_copies,)),
             pltpu.SemaphoreType.DMA((8,)),
             pltpu.SemaphoreType.DMA((8,)),
+            pltpu.SemaphoreType.DMA,
             pltpu.SemaphoreType.DMA,
             pltpu.SemaphoreType.DMA((NPLANE,)),
         ],
@@ -281,7 +304,7 @@
             flops=2 * 2048 * 2048 * WIN, bytes_accessed=6 * 1024 * 1024, transcendentals=0
         ),
         name="composites",
-    )(weights, library_t)
+    )(weights, library_t, kernels_t)
 
 
 BLOCKS = 32
@@ -305,7 +328,7 @@
         grid=(n_blocks // BLOCKS,),
         out_shape=jax.ShapeDtypeStruct((n_z, n_f, n_blocks * ROWS), jnp.bfloat16),
         in_specs=[
-            pl.BlockSpec((n_z, n_f, n_w), lambda i: (0, 0, 0)),
+            pl.BlockSpec(memory_space=pltpu.VMEM),
             pl.BlockSpec(memory_space=pltpu.VMEM),
         ],
         out_specs=pl.BlockSpec((n_z, n_f, BLOCKS * ROWS), lambda i: (0, 0, i)),
@@ -315,8 +338,9 @@
 
 
 def local(sfh_weights, library, kernels):
-    composite = composites(sfh_weights, library.T)
-    fluxes = photometry(kernels.transpose(0, 2, 1), composite)
+    inputs = (sfh_weights, library.T, kernels.transpose(0, 2, 1))
+    composite, kernels_t = composites(*[pltpu.with_memory_space_constraint(a, pltpu.HBM) for a in inputs])
+    fluxes = photometry(kernels_t, composite)
     return fluxes.transpose(0, 2, 1)
 
 

time: 81.3 us -> 77.6 us (0.954)
  local copies, waits for them, and re-layouts: 2.75 us -> 0 us
    unnamed x6 -> x0, local copies, waits for them, and re-layouts: 2.75 us -> none
where the time goes in v4:
time: 77.6 us; the launch traced here: 77.1 us
  Pallas kernels  77.1 us (99%)
    pallas_call x1, Pallas kernels, composites(): pl.pallas_call(gather_kernel, out_shape=[jax.ShapeDtypeStruct((NPLANE * N...  71.5 us
    pallas_call x1, Pallas kernels, photometry(): pl.pallas_call(photometry_kernel, grid=(n_blocks // BLOCKS,), out_shape=j...  5.54 us

profile of v4, /device:TPU:32, one launch (start us, length us, event | category | flops | bytes accessed | tf_op | source)
XLA Modules:
  0.0 77.1 jit_solution(2890420747188466959)
XLA Ops:
  0.0 71.5 %composites.1 = (bf16[128,160,128]{2,1,0:T(8,128)(2,1)S(1)}, bf16[5,64,160]{2,1,0:T(8,128)(2,1)S(1)}) custom-call(bf16[512,256]{1,0:T(8,128)(2,1)} %w_ref.1, bf16[160,256]{1,0:T(8,128)(2,1)} %bitcast.4, bf16[5,64,160]{2,1,0:T(8,128)(2,1)} %bitcast.3), custom_call_target="tpu_custom_call" | custom-call | flops 1342177280 | bytes 6291456 | tf_op jit(solution)/shard_map/composites/pallas_call | solution.py:280
  71.5 5.5 %photometry.1 = bf16[5,64,16384]{2,1,0:T(8,128)(2,1)} custom-call(bf16[5,64,160]{2,1,0:T(8,128)(2,1)S(1)} %get-tuple-element.7.k_ref, bf16[128,160,128]{2,1,0:T(8,128)(2,1)S(1)} %get-tuple-element.8.c_ref), custom_call_target="tpu_custom_call" | custom-call | tf_op jit(solution)/shard_map/photometry/pallas_call | solution.py:326

commit v5 on v4

--- a/solution.py
+++ b/solution.py
@@ -32,7 +32,7 @@
 FAR_FIRST = (2, 1, 3, 0)
 Z_SEND, Z_RECV = (-0.05, 1.0, 2.9), (2.85, 4.85, 8.8)
 LIBRARY, TURN, FIRST, PACE = 0.05, 0.8, 2.2, 0.65
-PAIR_LAG, RING_LAG, STORE_LAG = 2.0, 4.0, 6.0
+PAIR_LAG, RING_LAG, STORE_LAG = 2.0, 4.0, 10.0
 SETTLE = 0.5
 
 
@@ -307,7 +307,7 @@
     )(weights, library_t, kernels_t)
 
 
-BLOCKS = 32
+BLOCKS = 64
 
 
 def photometry_kernel(k_ref, c_ref, o_ref):

time: 77.6 us -> 77.6 us (level); the launches traced: 77.1 us -> 76.3 us
  Pallas kernels: 77.1 us -> 76.3 us
    pallas_call x1, Pallas kernels: 71.5 us -> 70.7 us  [composites(): pl.pallas_call(gather_kernel, out_shape=[jax.ShapeDtypeStruct((NPLANE * N...]
where the time goes in v5:
time: 77.6 us; the launch traced here: 76.3 us
  Pallas kernels  76.3 us (98%)
    pallas_call x1, Pallas kernels, composites(): pl.pallas_call(gather_kernel, out_shape=[jax.ShapeDtypeStruct((NPLANE * N...  70.7 us
    pallas_call x1, Pallas kernels, photometry(): pl.pallas_call(photometry_kernel, grid=(n_blocks // BLOCKS,), out_shape=j...  5.63 us

profile of v5, /device:TPU:32, one launch (start us, length us, event | category | flops | bytes accessed | tf_op | source)
XLA Modules:
  0.0 76.3 jit_solution(9666515987175263535)
XLA Ops:
  0.0 70.7 %composites.1 = (bf16[128,160,128]{2,1,0:T(8,128)(2,1)S(1)}, bf16[5,64,160]{2,1,0:T(8,128)(2,1)S(1)}) custom-call(bf16[512,256]{1,0:T(8,128)(2,1)} %w_ref.1, bf16[160,256]{1,0:T(8,128)(2,1)} %bitcast.4, bf16[5,64,160]{2,1,0:T(8,128)(2,1)} %bitcast.3), custom_call_target="tpu_custom_call" | custom-call | flops 1342177280 | bytes 6291456 | tf_op jit(solution)/shard_map/composites/pallas_call | solution.py:280
  70.7 5.6 %photometry.1 = bf16[5,64,16384]{2,1,0:T(8,128)(2,1)} custom-call(bf16[5,64,160]{2,1,0:T(8,128)(2,1)S(1)} %get-tuple-element.7.k_ref, bf16[128,160,128]{2,1,0:T(8,128)(2,1)S(1)} %get-tuple-element.8.c_ref), custom_call_target="tpu_custom_call" | custom-call | tf_op jit(solution)/shard_map/photometry/pallas_call | solution.py:326

commit v6 on v4

--- a/solution.py
+++ b/solution.py
@@ -32,7 +32,7 @@
 FAR_FIRST = (2, 1, 3, 0)
 Z_SEND, Z_RECV = (-0.05, 1.0, 2.9), (2.85, 4.85, 8.8)
 LIBRARY, TURN, FIRST, PACE = 0.05, 0.8, 2.2, 0.65
-PAIR_LAG, RING_LAG, STORE_LAG = 2.0, 4.0, 6.0
+PAIR_LAG, RING_LAG, STORE_LAG = 2.0, 4.0, 8.0
 SETTLE = 0.5
 
 

time: 77.6 us -> 77.4 us (level)
  Pallas kernels: 77.1 us -> 76.2 us
    pallas_call x1, Pallas kernels: 71.5 us -> 70.7 us  [composites(): pl.pallas_call(gather_kernel, out_shape=[jax.ShapeDtypeStruct((NPLANE * N...]
where the time goes in v6:
time: 77.4 us; the launch traced here: 76.2 us
  Pallas kernels  76.2 us (98%)
    pallas_call x1, Pallas kernels, composites(): pl.pallas_call(gather_kernel, out_shape=[jax.ShapeDtypeStruct((NPLANE * N...  70.7 us
    pallas_call x1, Pallas kernels, photometry(): pl.pallas_call(photometry_kernel, grid=(n_blocks // BLOCKS,), out_shape=j...  5.54 us

profile of v6, /device:TPU:32, one launch (start us, length us, event | category | flops | bytes accessed | tf_op | source)
XLA Modules:
  0.0 76.2 jit_solution(17344296899321168535)
XLA Ops:
  0.0 70.7 %composites.1 = (bf16[128,160,128]{2,1,0:T(8,128)(2,1)S(1)}, bf16[5,64,160]{2,1,0:T(8,128)(2,1)S(1)}) custom-call(bf16[512,256]{1,0:T(8,128)(2,1)} %w_ref.1, bf16[160,256]{1,0:T(8,128)(2,1)} %bitcast.4, bf16[5,64,160]{2,1,0:T(8,128)(2,1)} %bitcast.3), custom_call_target="tpu_custom_call" | custom-call | flops 1342177280 | bytes 6291456 | tf_op jit(solution)/shard_map/composites/pallas_call | solution.py:280
  70.7 5.5 %photometry.1 = bf16[5,64,16384]{2,1,0:T(8,128)(2,1)} custom-call(bf16[5,64,160]{2,1,0:T(8,128)(2,1)S(1)} %get-tuple-element.7.k_ref, bf16[128,160,128]{2,1,0:T(8,128)(2,1)S(1)} %get-tuple-element.8.c_ref), custom_call_target="tpu_custom_call" | custom-call | tf_op jit(solution)/shard_map/photometry/pallas_call | solution.py:326
